TPU v7x, 32 devices: a whole 2x2x4 slice. The times are simulated.
32 devices in a mesh: space: 16 (over z, y, x), dp: 2 (over core).
Axes of the slice: x: 2, y: 2, z: 4, core: 2. Of those that a mesh axis runs over, the one named last changes fastest.
Arguments:
- volumes: bfloat16 [2, 4, 64, 32, 32], P('dp', None, 'space'), may hold values from -6 to 6
- kernel_one: bfloat16 [32, 4, 3, 3, 3], replicated, may hold values from -0.625 to 0.625
- kernel_two: bfloat16 [64, 32, 3, 3, 3], replicated, may hold values from -0.21875 to 0.21875
- cotangent: bfloat16 [2, 64, 32, 256], P('dp', None, 'space'), may hold values from -6 to 6
Outputs:
- features: bfloat16 [2, 64, 32, 256], P('dp', None, 'space')
- pooled_grad: bfloat16 [2, 32, 32, 256], P('dp', None, 'space')
- grad_one: float32 [3456], P('space')
- grad_two: float32 [55296], P('space')
All inputs are finite; a program needn't handle non-finite values.
Results may differ from a plain program's by a relative error of at most 0.006.
Values may be sent and summed in bfloat16 or wider, within the bound.
No kernel may reach another device: no remote copies, remote signals or barrier semaphores. Data moves between devices by JAX's collectives and lax.ppermute only.
A program may use at most 64 MiB of HBM per device.

v0:
```python
import functools
import math

import jax
import jax.numpy as jnp
import numpy as np
from jax import lax
from jax.experimental import pallas as pl
from jax.experimental.pallas import tpu as pltpu
from jax.sharding import PartitionSpec as P

F32 = jnp.float32
BF16 = jnp.bfloat16
SHIFTS = [(dy, dx) for dy in (-1, 0, 1) for dx in (-1, 0, 1)]
NN = (((1,), (0,)), ((), ()))
NT = (((1,), (1,)), ((), ()))
LANES = 1024
HALF = 512
ONE_AT = 896


def dot(a, b, dims=NN):
    return lax.dot_general(a, b, dims, preferred_element_type=F32)


def inside(cells, width):
    lane = lax.broadcasted_iota(jnp.int32, (1, cells), 1)
    col, row = lane & (width - 1), lax.shift_right_logical(lane, width.bit_length() - 1)

    def factor(pos, step):
        if step == 0:
            return None
        return jnp.where(pos < width - 1 if step > 0 else pos > 0, 1.0, 0.0)

    return [(factor(col, d), factor(row, d)) for d in (-1, 0, 1)]


def moved_by(field, move, factor):
    return field if move == 0 else pltpu.roll(field, (-move) % field.shape[1], 1) * factor


def all_shifts(field, width):
    factors = [
        [f if f is None else f.astype(field.dtype) for f in pair]
        for pair in inside(field.shape[1], width)
    ]
    across = [moved_by(field, dx, factors[dx + 1][0]) for dx in (-1, 0, 1)]
    return [moved_by(across[dx + 1], dy * width, factors[dy + 1][1]) for dy, dx in SHIFTS]


def pool_pattern():
    cell = lax.broadcasted_iota(jnp.int32, (512, 128), 0)
    block = lax.broadcasted_iota(jnp.int32, (512, 128), 1)
    at = 16 * lax.shift_right_logical(cell, 6) + lax.shift_right_logical(cell & 31, 1)
    return jnp.where(at == block, 0.125, 0.0).astype(BF16)


def silu_parts(v):
    s = 0.5 + 0.5 * jnp.tanh(0.5 * v)
    return v * s, s


def band_maps():
    to_kernel = np.zeros((4, 256, 108), np.float32)
    to_flat = np.zeros((4, 256, 128), np.float32)
    for p in range(4):
        for s in range(9):
            for dz in range(3):
                q = p + dz - 1
                for ci in range(4):
                    if 0 <= q <= 3:
                        row = 16 * s + 4 * q + ci
                    else:
                        row = 144 + 8 * s + (0 if q < 0 else 4) + ci
                    tap = 9 * dz + s
                    to_kernel[p, row, 4 * tap + ci] = 1
                    to_flat[p, row, 64 * (ci // 2) + 27 * (ci % 2) + tap] = 1
    return to_kernel, to_flat.reshape(1024, 128)


def prepare_body(
    vol_hbm, cot_hbm, *refs,
):
    weights, (next_ref, near_ref, far_next_ref, far_near_ref) = refs[:4], refs[4:8]
    kept, (vol_ref, cot_ref, cells_ref, sems) = refs[8:12], refs[12:]
    me = lax.axis_index("space")
    odd, upper = me % 2 == 1, (me // 2) % 2 == 1
    vol_copy = pltpu.make_async_copy(vol_hbm, vol_ref, sems.at[0])
    cot_copy = pltpu.make_async_copy(cot_hbm, cot_ref, sems.at[1])
    vol_copy.start()
    cot_copy.start()
    copies = [
        pltpu.make_async_copy(src, dst, sems.at[2 + i])
        for i, (src, dst) in enumerate(zip(weights, kept))
    ]
    for copy in copies:
        copy.start()
    vol_copy.wait()
    cin, planes, width = vol_ref.shape[1:4]
    for plane in range(planes):
        for ch in range(cin):
            at = (plane * cin + ch) * width
            cells_ref[at : at + width] = vol_ref[0, ch, plane].astype(F32)
    count = planes * cin
    blocks = []
    for b in range(4):
        lines = [cells_ref[pl.ds(8 * b + y, count, stride=width), :] for y in range(8)]
        rows = jnp.concatenate(lines, axis=1)
        near_ref[count * b : count * b + count] = rows.astype(BF16)
        next_ref[count * b : count * b + count] = rows.astype(BF16)
        blocks.append(rows)
    halves = [jnp.concatenate(blocks[2 * m : 2 * m + 2], axis=1) for m in range(2)]
    top = lax.broadcasted_iota(jnp.int32, (8, HALF), 0) < 4
    first = jnp.where(top, halves[0][0:8], pltpu.roll(halves[1][0:8], 4, 0))
    last = jnp.where(top, pltpu.roll(halves[0][8:16], 4, 0), halves[1][8:16])
    far_near_ref[...] = jnp.where(upper, first, last).astype(BF16)
    far_next_ref[...] = jnp.where(upper, last, first).astype(BF16)
    cot_copy.wait()
    cot = cot_ref[0].astype(F32)
    cots = (cot[:, 0, :], cot[:, 1, :])
    near_ref[64:128] = jnp.where(odd, cots[0], cots[1]).astype(BF16)
    next_ref[64:128] = jnp.where(odd, cots[1], cots[0]).astype(BF16)
    for copy in copies:
        copy.wait()


def sum_body(parts_ref, total_ref):
    total = parts_ref[0].astype(F32)
    for i in range(1, parts_ref.shape[0]):
        total = total + parts_ref[i].astype(F32)
    total_ref[...] = total


def finish_body(mine_ref, other_ref, one_ref, two_ref):
    total = mine_ref[...] + other_ref[...]
    share = total.shape[0] // 2
    total = jnp.concatenate([total[0:share], total[share:]], axis=1)
    two_ref[...] = jnp.concatenate([total[r, 0:864] for r in range(share)])
    one = total[:, ONE_AT : ONE_AT + 54] + total[:, ONE_AT + 64 : ONE_AT + 118]
    one_ref[...] = jnp.concatenate([one[r] for r in range(share)])


def unfold(block, rows):
    return jnp.concatenate([block[rows * b : rows * b + rows] for b in range(4)], axis=1)


def pool_sums(sums, pattern):
    rows = sums.shape[0]
    high = sums.astype(BF16)
    low = (sums - high.astype(F32)).astype(BF16)
    halves = [part[:, 512 * m : 512 * m + 512] for part in (high, low) for m in range(2)]
    out = dot(jnp.concatenate(halves, axis=0), pattern)
    out = out[0 : 2 * rows] + out[2 * rows : 4 * rows]
    return jnp.concatenate([out[0:rows], out[rows : 2 * rows]], axis=1)


def spread_cells(field, pattern):
    rows = field.shape[0]
    high = field.astype(BF16)
    low = (field - high.astype(F32)).astype(BF16)
    halves = [part[:, 128 * m : 128 * m + 128] for part in (high, low) for m in range(2)]
    out = dot(jnp.concatenate(halves, axis=0), pattern, NT)
    out = out[0 : 2 * rows] + out[2 * rows : 4 * rows]
    return jnp.concatenate([out[0:rows], out[rows : 2 * rows]], axis=1)


def spread_taps(taps, half):
    factors = inside(half * half, half)
    total = None
    for dx in (-1, 0, 1):
        column = None
        for dy in (-1, 0, 1):
            s = 3 * (1 - dy) + (1 - dx)
            part = moved_by(taps[32 * s : 32 * s + 32], dy * half, factors[dy + 1][1])
            column = part if column is None else column + part
        column = moved_by(column, dx, factors[dx + 1][0])
        total = column if total is None else total + column
    return total


def inner_body(
    count,
    own_next_ref, own_near_ref, next_ref, near_ref, k1_ref, k2_ref, to_kernel_ref, to_flat_ref,
    feat_ref, send_ref, part_ref, pre_ref, act_ref, pre_two_ref, far_one_ref, far_two_ref,
    term_ref, pair_ref, rows_ref, out_ref,
):
    slabs = lax.axis_size("space")
    me = lax.axis_index("space")
    half = 16

    odd = me % 2 == 1
    own = unfold(own_near_ref[0:64].astype(F32), 16)
    near, following = near_ref[0:64].astype(F32), next_ref[0:64].astype(F32)
    left = unfold(jnp.where(odd, near, following), 16)
    right = unfold(jnp.where(odd, following, near), 16)
    top = lax.broadcasted_iota(jnp.int32, (8, LANES), 0) < 4
    edges = (
        jnp.where(top, 0.0, pltpu.roll(own[0:8], 4, 0)),
        jnp.where(top, pltpu.roll(left[8:16], 4, 0), pltpu.roll(right[0:8], 4, 0)),
        jnp.where(top, pltpu.roll(own[8:16], 4, 0), 0.0),
    )
    moved_edges = all_shifts(jnp.concatenate(edges, axis=0), 2 * half)
    moved = all_shifts(jnp.concatenate([left, own, right], axis=0).astype(BF16), 2 * half)
    patches = []
    for g in range(3):
        rows = [m[8 * g : 8 * g + 8] for m in moved_edges] + [jnp.zeros((40, LANES), F32)]
        rows = jnp.concatenate(rows, axis=0).astype(BF16)
        patches.append(jnp.concatenate([*(m[16 * g : 16 * g + 16] for m in moved), rows], axis=0))

    k1t = k1_ref[...].astype(F32).reshape(108, 32).T.astype(BF16)
    two_by_dz = jnp.concatenate(
        [k2_ref[288 * dz : 288 * dz + 288].astype(F32).T for dz in range(3)], axis=0
    ).astype(BF16)
    banded = jnp.concatenate(
        [dot(k1t, to_kernel_ref[p], NT).astype(BF16) for p in range(4)], axis=0
    )
    far_one_ref[...] = jnp.concatenate(
        [dot(k1t, to_kernel_ref[p, 144:216], NT).astype(BF16) for p in (0, 3)], axis=0
    )
    far_two_ref[0] = two_by_dz[0:64]
    far_two_ref[1] = two_by_dz[128:192]
    pattern = pool_pattern()

    pre = dot(banded, patches[0])
    pre_ref[0:32] = pre[0:32]
    act, s = silu_parts(pre[32:128])
    act_ref[0:32] = act[0:32]
    slopes = [(s + act * (1.0 - s))[32:96]]
    sums = [act[32:64] + act[64:96]]
    act, s = silu_parts(dot(banded, patches[1]))
    slopes.append(s + act * (1.0 - s))
    sums += [act[0:32] + act[32:64], act[64:96] + act[96:128]]
    pre = dot(banded, patches[2])
    pre_ref[32:64] = pre[96:128]
    act, s = silu_parts(pre[0:96])
    act_ref[32:64] = act[64:96]
    slopes.append((s + act * (1.0 - s))[0:64])
    sums += [act[0:32] + act[32:64]]
    pooled = pool_sums(jnp.concatenate(sums, axis=0), pattern)
    plane = lax.shift_right_logical(lax.broadcasted_iota(jnp.int32, pooled.shape, 0), 5)
    real = ((plane > 0) | (me > 0)) & ((plane < 3) | (me < slabs - 1))
    pooled = jnp.where(real, pooled, 0.0).astype(BF16)

    moved = all_shifts(pooled, half)
    planes = [jnp.concatenate([m[32 * q : 32 * q + 32] for m in moved], axis=0) for q in range(4)]
    pre_two = [None] * 4
    for q, columns in enumerate(planes):
        by_dz = dot(two_by_dz, columns)
        for dz in range(3):
            p = q + 1 - dz
            if 0 <= p < 4:
                part = by_dz[64 * dz : 64 * dz + 64]
                pre_two[p] = part if pre_two[p] is None else pre_two[p] + part
    pre_two_ref[0], pre_two_ref[1] = pre_two[0], pre_two[3]

    own_cots = own_near_ref[64:128].astype(F32), own_next_ref[64:128].astype(F32)
    cots = jnp.where(odd, *own_cots), jnp.where(odd, *own_cots[::-1])
    deltas = []
    for p in range(2):
        act, s = silu_parts(pre_two[p + 1])
        feat_ref[p] = act.astype(BF16)
        deltas.append((cots[p] * (s + act * (1.0 - s))).astype(BF16))

    share = 64 // slabs

    def place(columns, at):
        for first in range(0, columns.shape[1], 128):
            tile = (at + first) % HALF // 128
            rows_ref[tile] = columns[:, first : first + 128]
            for r in range(share):
                target = pl.ds((at + first) // HALF * share + r, slabs, stride=2 * share)
                out_ref[tile, target, :] = rows_ref[tile, pl.ds(r, slabs, stride=share), :]

    columns = [jnp.concatenate(planes[p : p + 3], axis=0) for p in range(2)]
    term = dot(columns[0], deltas[0], NT) + dot(columns[1], deltas[1], NT)
    term_ref[...] = term * (1.0 / math.sqrt(count // 8))
    rows = jnp.concatenate([term_ref[pl.ds(ch, 27, stride=32), :] for ch in range(32)], axis=0)
    place(rows[0:HALF].T, 0)
    rows = jnp.concatenate([rows[HALF:864], jnp.zeros((ONE_AT - 864, 64), F32)], axis=0)
    place(rows.T, HALF)

    grads = []
    for p in range(-1, 3):
        sources = [q for q in range(2) if abs(q - p) < 2]
        taps = [k2_ref[288 * (1 + p - q) : 288 * (1 + p - q) + 288] for q in sources]
        given = jnp.concatenate([deltas[q] for q in sources], axis=0)
        grads.append(spread_taps(dot(jnp.concatenate(taps, axis=1), given), half))
    part_ref[0], part_ref[1] = grads[1], grads[2]

    grads = jnp.where(real, jnp.concatenate(grads, axis=0), 0.0)
    spread = spread_cells(grads, pattern)
    spread = [spread[32 * q : 32 * q + 32] for q in range(4)]
    wide = []
    for g, under in enumerate(((0,), (1, 2), (3,))):
        field = jnp.concatenate([spread[q] for q in under for _ in range(2)], axis=0)
        wide.append(dot((field * slopes[g]).astype(BF16), patches[g], NT))
    wide = wide[1] + jnp.concatenate([wide[2], wide[0]], axis=0)
    wide = jnp.concatenate([wide[32 * p : 32 * p + 32] for p in range(4)], axis=1)
    high = wide.astype(BF16)
    low = (wide - high.astype(F32)).astype(BF16)
    term_one = dot(jnp.concatenate([high, low], axis=0), to_flat_ref[...])
    term_one = (term_one[0:32] + term_one[32:64]) * (1.0 / math.sqrt(count))
    for h, half_row in enumerate((term_one, pltpu.roll(term_one, 64, 1))):
        pair_ref[pl.ds(h, 32, stride=2), :] = half_row
    rows = pair_ref[...]
    rounded = rows.astype(BF16).astype(F32)
    lane = lax.broadcasted_iota(jnp.int32, rows.shape, 1)
    pair = jnp.where(lane < 64, rounded, pltpu.roll(rows - rounded, 64, 1))
    place(pair, ONE_AT)
    for tile in range(4):
        send_ref[:, 128 * tile : 128 * tile + 128] = out_ref[tile].astype(BF16)


def outer_body(
    far_next_ref, far_near_ref, next_ref, near_ref, k2_ref,
    feat_ref, part_ref, pre_ref, act_ref, pre_two_ref, far_one_ref, far_two_ref,
    feat_out, pgrad_out,
):
    slabs = lax.axis_size("space")
    me = lax.axis_index("space")
    half = 16
    odd, upper = me % 2 == 1, (me // 2) % 2 == 1
    pattern = pool_pattern()
    far_near, far_next = far_near_ref[...].astype(F32), far_next_ref[...].astype(F32)
    far_left, far_right = jnp.where(upper, far_near, far_next), jnp.where(upper, far_next, far_near)
    top = lax.broadcasted_iota(jnp.int32, (8, LANES), 0) < 4
    edge = jnp.where(
        top,
        jnp.concatenate([far_left, pltpu.roll(far_left, 4, 0)], axis=1),
        jnp.concatenate([pltpu.roll(far_right, 4, 0), far_right], axis=1),
    )
    patches = jnp.concatenate(all_shifts(edge, 2 * half), axis=0).astype(BF16)
    act, _ = silu_parts(pre_ref[...] + dot(far_one_ref[...], patches))
    pooled = pool_sums(act_ref[...] + act, pattern)
    plane = lax.shift_right_logical(lax.broadcasted_iota(jnp.int32, pooled.shape, 0), 5)
    real = ((plane > 0) | (me > 0)) & ((plane < 1) | (me < slabs - 1))
    pooled = jnp.where(real, pooled, 0.0).astype(BF16)
    moved = all_shifts(pooled, half)

    near, following = near_ref[64:128].astype(F32), next_ref[64:128].astype(F32)
    cots = jnp.where(odd, near, following), jnp.where(odd, following, near)
    for p in range(2):
        columns = jnp.concatenate([m[32 * p : 32 * p + 32] for m in moved], axis=0)
        pre = pre_two_ref[p] + dot(far_two_ref[p], columns)
        act, s = silu_parts(pre)
        delta = (cots[p] * (s + act * (1.0 - s))).astype(BF16)
        taps = dot(k2_ref[576 * (1 - p) : 576 * (1 - p) + 288], delta)
        pgrad_out[0, :, p, :] = (part_ref[p] + spread_taps(taps, half)).astype(BF16)
        feat_out[0, :, p, :] = feat_ref[p]


def on_device(volumes, kernel_one, kernel_two, cotangent):
    _, cin, planes, width, _ = volumes.shape
    half = width // 2
    slabs = lax.axis_size("space")
    copies = lax.axis_size("dp")
    count = copies * planes * slabs * width * width

    to_kernel, to_flat = band_maps()
    weights = (
        jnp.transpose(kernel_one, (2, 3, 4, 1, 0)).reshape(27, 4, 32),
        jnp.transpose(kernel_two, (2, 3, 4, 1, 0)).reshape(864, 64),
        jnp.asarray(to_kernel, BF16),
        jnp.asarray(to_flat, BF16),
    )

    def in_hbm(*arrays):
        return [pltpu.with_memory_space_constraint(x, pltpu.HBM) for x in arrays]

    inputs = in_hbm(volumes, cotangent, *weights)
    hbm = pl.BlockSpec(memory_space=pltpu.HBM)
    limit = pltpu.CompilerParams(vmem_limit_bytes=48 * 1024 * 1024)
    whole = jax.ShapeDtypeStruct((128, width * width // 4), BF16)
    part = jax.ShapeDtypeStruct((2 * cin, width * width // 2), BF16)
    to_next, to_near, to_far_next, to_far_near, *weights = pl.pallas_call(
        prepare_body,
        out_shape=(
            whole, whole, part, part, *(jax.ShapeDtypeStruct(w.shape, BF16) for w in weights)
        ),
        in_specs=[hbm] * len(inputs),
        scratch_shapes=[
            pltpu.VMEM(volumes.shape, BF16),
            pltpu.VMEM(cotangent.shape, BF16),
            pltpu.VMEM((planes * cin * width, width), F32),
            pltpu.SemaphoreType.DMA((len(inputs),)),
        ],
        compiler_params=limit,
    )(*inputs)

    def swap(block, pairs):
        pairs = [p for p in pairs if max(p) < slabs]
        return lax.ppermute(block, "space", pairs + [(t, f) for f, t in pairs])

    evens = range(0, slabs, 2)
    fours = [i + j for i in range(0, slabs, 4) for j in range(2)]
    following = swap(to_next, [(i + 1, i + 2) for i in evens])
    near = swap(to_near, [(i, i + 1) for i in evens])
    far_next = swap(to_far_next, [(i + 2, i + 4) for i in fours])

    cells = half * half
    shapes = {
        "features": ((2, 64, cells), BF16),
        "send": ((128, HALF), BF16),
        "part": ((2, 32, cells), F32),
        "pre": ((64, LANES), F32),
        "act": ((64, LANES), F32),
        "pre_two": ((2, 64, cells), F32),
        "far_one": ((64, 72), BF16),
        "far_two": ((2, 64, 288), BF16),
    }
    feat, send, *inner = pl.pallas_call(
        functools.partial(inner_body, count),
        out_shape=tuple(jax.ShapeDtypeStruct(*x) for x in shapes.values()),
        scratch_shapes=[
            pltpu.VMEM(shape, F32) for shape in ((864, 64), (64, 128), (4, 64, 128), (4, 128, 128))
        ],
        compiler_params=limit,
        cost_estimate=pl.CostEstimate(flops=2 * 10**10, bytes_accessed=2 * 10**6, transcendentals=10**6),
    )(to_next, to_near, following, near, *weights)
    share = 64 // slabs
    send, far_next = lax.optimization_barrier((send.reshape(slabs, 2 * share, HALF), far_next))
    send = pltpu.with_memory_space_constraint(send, pltpu.VMEM)
    parts = lax.all_to_all(send, "space", 0, 0, tiled=True)
    _, to_far_near = lax.optimization_barrier((send, to_far_near))
    far_near = swap(to_far_near, [(i, i + 2) for i in fours])
    features, pooled_grad = pl.pallas_call(
        outer_body,
        out_shape=(
            jax.ShapeDtypeStruct((1, 64, 2, cells), BF16),
            jax.ShapeDtypeStruct((1, 32, 2, cells), BF16),
        ),
        compiler_params=limit,
        cost_estimate=pl.CostEstimate(flops=2 * 10**9, bytes_accessed=10**6, transcendentals=10**5),
    )(far_next, far_near, following, near, weights[1], feat, *inner)
    parts, features, pooled_grad = lax.optimization_barrier((parts, features, pooled_grad))
    total = pl.pallas_call(
        sum_body,
        out_shape=jax.ShapeDtypeStruct(parts.shape[1:], F32),
        compiler_params=limit,
    )(parts)

    def other_core(block, step):
        return lax.ppermute(block, "dp", [(i, i ^ step) for i in range(copies)])

    step = 1
    while 2 * step < copies:
        total = total + other_core(total, step)
        step *= 2
    other = other_core(total, step)
    grad_one, grad_two = pl.pallas_call(
        finish_body,
        out_shape=(jax.ShapeDtypeStruct((share * 54,), F32), jax.ShapeDtypeStruct((share * 864,), F32)),
        compiler_params=limit,
    )(total, other)
    return (features, pooled_grad, grad_one, grad_two)


def solution(mesh):
    in_specs = (P("dp", None, "space", None, None), P(), P(), P("dp", None, "space", None))
    out_specs = (P("dp", None, "space", None), P("dp", None, "space", None), P("space"), P("space"))
    return jax.shard_map(
        on_device, mesh=mesh, in_specs=in_specs, out_specs=out_specs, check_vma=False
    )
```

profile of v0, /device:TPU:0, one launch (start us, length us, event | category | flops | bytes accessed | tf_op | source)
XLA Modules:
  0.0 32.1 jit_solution(16505289501061385450)
XLA Ops:
  0.6 1.4 %shard_map.93 = (bf16[128,256]{1,0:T(8,128)(2,1)S(1)}, bf16[128,256]{1,0:T(8,128)(2,1)S(1)}, bf16[8,512]{1,0:T(8,128)(2,1)S(1)}, bf16[8,512]{1,0:T(8,128)(2,1)S(...) custom-call(bf16[1,4,4,32,32]{4,3,2,1,0:T(8,128)(2,1)} %vol_hbm.1, ...), custom_call_target="tpu_custom_call" | custom-call | tf_op jit(solution)/shard_map/pallas_call | solution.py:375
  2.0 0.7 %collective-permute-start = (bf16[128,256]{1,0:T(8,128)(2,1)S(1)}, bf16[128,256]{1,0:T(8,128)(2,1)S(1)}, u32[]{:S(2)}, u32[]{:S(2)}) collective-permute-start(bf16[128,256]{1,0:T(8,128)(2,1)S(1)} %get-tuple-element.30.own_next_ref), channel_id=1, source_target_pairs={{2,4},{6,8},{10,12},{14,16},{18,20},{22,24},{26,28},{4,2},{8,6},{1... | collective-permute-start | bytes 196616 | tf_op jit(solution)/shard_map/ppermute | solution.py:392
  2.7 5.7 %collective-permute-start.1 = (bf16[128,256]{1,0:T(8,128)(2,1)S(1)}, bf16[128,256]{1,0:T(8,128)(2,1)S(1)}, u32[]{:S(2)}, u32[]{:S(2)}) collective-permute-start(bf16[128,256]{1,0:T(8,128)(2,1)S(1)} %get-tuple-element.31.own_near_ref), channel_id=1, source_target_pairs={{0,2},{4,6},{8,10},{12,14},{16,18},{20,22},{24,26},{28,30},{2,0},{... | collective-permute-start | bytes 196616 | tf_op jit(solution)/shard_map/ppermute | solution.py:392
  8.4 0.6 %collective-permute-start.2 = (bf16[8,512]{1,0:T(8,128)(2,1)S(1)}, bf16[8,512]{1,0:T(8,128)(2,1)S(1)}, u32[]{:S(2)}, u32[]{:S(2)}) collective-permute-start(bf16[8,512]{1,0:T(8,128)(2,1)S(1)} %get-tuple-element.37), channel_id=1, source_target_pairs={{4,8},{6,10},{12,16},{14,18},{20,24},{22,26},{8,4},{10,6},{16,12},... | collective-permute-start | bytes 24584 | tf_op jit(solution)/shard_map/ppermute | solution.py:392
  9.1 0.0 collective-permute-done.next_ref
  9.1 2.5 %collective-permute-done.1.near_ref = bf16[128,256]{1,0:T(8,128)(2,1)S(1)} collective-permute-done((bf16[128,256]{1,0:T(8,128)(2,1)S(1)}, bf16[128,256]{1,0:T(8,128)(2,1)S(1)}, u32[]{:S(2)}, u32[]{:S(2)}) %collective-permute-start.1) | collective-permute-done | bytes 65568 | tf_op jit(solution)/shard_map/ppermute | solution.py:392
  11.6 4.7 %shard_map.94 = (bf16[2,64,256]{2,1,0:T(8,128)(2,1)S(1)}, bf16[128,512]{1,0:T(8,128)(2,1)}, f32[2,32,256]{2,1,0:T(8,128)S(1)}, f32[64,1024]{1,0:T(8,128)S(1)}, f...) custom-call(bf16[128,256]{1,0:T(8,128)(2,1)S(1)} %get-tuple-element., ...), custom_call_target="tpu_custom_call" | custom-call | flops 20000000000 | bytes 2000000 | tf_op jit(solution)/shard_map/pallas_call | solution.py:411
  16.2 0.0 collective-permute-done.2.far_next_ref
  16.2 6.1 %all-to-all-start = ((bf16[16,8,512]{2,1,0:T(8,128)(2,1)}), bf16[16,8,512]{2,1,0:T(8,128)(2,1)S(1)}, u32[]{:S(2)}, u32[]{:S(2)}) async-start(bf16[16,8,512]{2,1,0:T(8,128)(2,1)} %bitcast.4), calls=%async_computation | async-start | bytes 262144 | tf_op jit(solution)/shard_map/all_to_all | solution.py:423
  22.3 1.9 %collective-permute-start.3 = (bf16[8,512]{1,0:T(8,128)(2,1)S(1)}, bf16[8,512]{1,0:T(8,128)(2,1)S(1)}, u32[]{:S(2)}, u32[]{:S(2)}) collective-permute-start(bf16[8,512]{1,0:T(8,128)(2,1)S(1)} %get-tuple-element.41), channel_id=1, source_target_pairs={{0,4},{2,6},{8,12},{10,14},{16,20},{18,22},{24,28},{26,30},{4,0},{... | collective-permute-start | bytes 24584 | tf_op jit(solution)/shard_map/ppermute | solution.py:392
  24.2 2.0 %collective-permute-done.3.far_near_ref = bf16[8,512]{1,0:T(8,128)(2,1)S(1)} collective-permute-done((bf16[8,512]{1,0:T(8,128)(2,1)S(1)}, bf16[8,512]{1,0:T(8,128)(2,1)S(1)}, u32[]{:S(2)}, u32[]{:S(2)}) %collective-permute-start.3) | collective-permute-done | bytes 8224 | tf_op jit(solution)/shard_map/ppermute | solution.py:392
  26.2 2.1 %shard_map.95 = (bf16[1,64,2,256]{3,2,1,0:T(2,128)(2,1)}, bf16[1,32,2,256]{3,2,1,0:T(2,128)(2,1)}) custom-call(bf16[8,512]{1,0:T(8,128)(2,1)S(1)} %collective-permute-done.2.far_next_ref, bf16[8,512]{1,0:T(8,128)(2,1)S(1)} %collective-permute-done.3.far_near_ref, bf16[128,256]{1,0:T(8,128)(2,1)S(1)} %collective-permute-done.next_ref, ...), custom_call_target="tpu_custom_call" | custom-call | flops 2000000000 | bytes 1000000 | tf_op jit(solution)/shard_map/pallas_call | solution.py:426
  28.3 1.7 %all-to-all-done.parts_ref = bf16[16,8,512]{2,1,0:T(8,128)(2,1)S(1)} async-done(((bf16[16,8,512]{2,1,0:T(8,128)(2,1)}), bf16[16,8,512]{2,1,0:T(8,128)(2,1)S(1)}, u32[]{:S(2)}, u32[]{:S(2)}) %all-to-all-start) | async-done | bytes 131104 | tf_op jit(solution)/shard_map/all_to_all | solution.py:423
  30.1 0.1 collective-permute-start.4
  30.2 1.2 %collective-permute-done.4.other_ref = f32[8,512]{1,0:T(8,128)S(1)} collective-permute-done((f32[8,512]{1,0:T(8,128)S(1)}, f32[8,512]{1,0:T(8,128)S(1)}, u32[]{:S(2)}, u32[]{:S(2)}) %collective-permute-start.4) | collective-permute-done | bytes 16416 | tf_op jit(solution)/shard_map/ppermute | solution.py:443
  31.4 0.7 %shard_map.97 = (f32[216]{0:T(256)}, f32[3456]{0:T(1024)}) custom-call(f32[8,512]{1,0:T(8,128)S(1)} %shard_map.96.mine_ref, f32[8,512]{1,0:T(8,128)S(1)} %collective-permute-done.4.other_ref), custom_call_target="tpu_custom_call" | custom-call | tf_op jit(solution)/shard_map/pallas_call | solution.py:450
  (1 shorter events, 0.0 us)
Async XLA Ops:
  2.0 7.1 %collective-permute-start = (bf16[128,256]{1,0:T(8,128)(2,1)S(1)}, bf16[128,256]{1,0:T(8,128)(2,1)S(1)}, u32[]{:S(2)}, u32[]{:S(2)}) collective-permute-start(bf16[128,256]{1,0:T(8,128)(2,1)S(1)} %get-tuple-element.30.own_next_ref), channel_id=1, source_target_pairs={{2,4},{6,8},{10,12},{14,16},{18,20},{22,24},{26,28},{4,2},{8,6},{1... | collective-permute-start | bytes 196616 | tf_op jit(solution)/shard_map/ppermute | solution.py:392
  2.7 8.9 %collective-permute-start.1 = (bf16[128,256]{1,0:T(8,128)(2,1)S(1)}, bf16[128,256]{1,0:T(8,128)(2,1)S(1)}, u32[]{:S(2)}, u32[]{:S(2)}) collective-permute-start(bf16[128,256]{1,0:T(8,128)(2,1)S(1)} %get-tuple-element.31.own_near_ref), channel_id=1, source_target_pairs={{0,2},{4,6},{8,10},{12,14},{16,18},{20,22},{24,26},{28,30},{2,0},{... | collective-permute-start | bytes 196616 | tf_op jit(solution)/shard_map/ppermute | solution.py:392
  8.4 7.8 %collective-permute-start.2 = (bf16[8,512]{1,0:T(8,128)(2,1)S(1)}, bf16[8,512]{1,0:T(8,128)(2,1)S(1)}, u32[]{:S(2)}, u32[]{:S(2)}) collective-permute-start(bf16[8,512]{1,0:T(8,128)(2,1)S(1)} %get-tuple-element.37), channel_id=1, source_target_pairs={{4,8},{6,10},{12,16},{14,18},{20,24},{22,26},{8,4},{10,6},{16,12},... | collective-permute-start | bytes 24584 | tf_op jit(solution)/shard_map/ppermute | solution.py:392
  16.2 13.9 %all-to-all-start = ((bf16[16,8,512]{2,1,0:T(8,128)(2,1)}), bf16[16,8,512]{2,1,0:T(8,128)(2,1)S(1)}, u32[]{:S(2)}, u32[]{:S(2)}) async-start(bf16[16,8,512]{2,1,0:T(8,128)(2,1)} %bitcast.4), calls=%async_computation | async-start | bytes 262144 | tf_op jit(solution)/shard_map/all_to_all | solution.py:423
  22.3 3.9 %collective-permute-start.3 = (bf16[8,512]{1,0:T(8,128)(2,1)S(1)}, bf16[8,512]{1,0:T(8,128)(2,1)S(1)}, u32[]{:S(2)}, u32[]{:S(2)}) collective-permute-start(bf16[8,512]{1,0:T(8,128)(2,1)S(1)} %get-tuple-element.41), channel_id=1, source_target_pairs={{0,4},{2,6},{8,12},{10,14},{16,20},{18,22},{24,28},{26,30},{4,0},{... | collective-permute-start | bytes 24584 | tf_op jit(solution)/shard_map/ppermute | solution.py:392
  30.1 1.2 %collective-permute-start.4 = (f32[8,512]{1,0:T(8,128)S(1)}, f32[8,512]{1,0:T(8,128)S(1)}, u32[]{:S(2)}, u32[]{:S(2)}) collective-permute-start(f32[8,512]{1,0:T(8,128)S(1)} %shard_map.96.mine_ref), channel_id=1, source_target_pairs={{0,1},{1,0},{2,3},{3,2},{4,5},{5,4},{6,7},{7,6},{8,9},{9,8},{10,11... | collective-permute-start | bytes 49160 | tf_op jit(solution)/shard_map/ppermute | solution.py:443
where the time goes:
time: 32.3 us; the launch traced here: 32.1 us
  starting transfers between devices  15.1 us (47%)
  Pallas kernels  8.9 us (28%)
  waiting for transfers between devices  7.38 us (23%)
  between operations  0.69 us (2%)
    ppermute x4, starting transfers between devices, swap(): return lax.ppermute(block, 'space', pairs + [(t, f) for f, t in pairs])  8.98 us
    all_to_all x1, starting transfers between devices, on_device(): parts = lax.all_to_all(send, 'space', 0, 0, tiled=True)  6.06 us
    pallas_call x1, Pallas kernels, on_device(): pl.pallas_call(functools.partial(inner_body, count), out_shape=tuple((jax...  4.66 us
    ppermute x4, waiting for transfers between devices, swap(): return lax.ppermute(block, 'space', pairs + [(t, f) for f, t in pairs])  4.47 us
    pallas_call x1, Pallas kernels, on_device(): pl.pallas_call(outer_body, out_shape=(jax.ShapeDtypeStruct((1, 64, 2, cel...  2.12 us
    all_to_all x1, waiting for transfers between devices, on_device(): parts = lax.all_to_all(send, 'space', 0, 0, tiled=True)  1.74 us
    pallas_call x1, Pallas kernels, on_device(): pl.pallas_call(prepare_body, out_shape=(whole, whole, part, part, *(jax.S...  1.39 us
    ppermute x1, waiting for transfers between devices, other_core(): return lax.ppermute(block, 'dp', [(i, i ^ step) for i in range(copies)])  1.17 us
  transfers between devices with their start and end apart: 6, of which 4 were waited for; matrix products, arithmetic and copies ran while one was open for 0% of the time, Pallas kernels for 21%

commit v1 on v0

--- a/solution.py
+++ b/solution.py
@@ -158,9 +158,11 @@
     rows = field.shape[0]
     high = field.astype(BF16)
     low = (field - high.astype(F32)).astype(BF16)
-    halves = [part[:, 128 * m : 128 * m + 128] for part in (high, low) for m in range(2)]
-    out = dot(jnp.concatenate(halves, axis=0), pattern, NT)
-    out = out[0 : 2 * rows] + out[2 * rows : 4 * rows]
+    halves = [
+        jnp.concatenate([part[:, 128 * m : 128 * m + 128] for part in (high, low)], axis=1)
+        for m in range(2)
+    ]
+    out = dot(jnp.concatenate(halves, axis=0), jnp.concatenate([pattern, pattern], axis=1), NT)
     return jnp.concatenate([out[0:rows], out[rows : 2 * rows]], axis=1)
 
 
@@ -271,13 +273,15 @@
                 target = pl.ds((at + first) // HALF * share + r, slabs, stride=2 * share)
                 out_ref[tile, target, :] = rows_ref[tile, pl.ds(r, slabs, stride=share), :]
 
-    columns = [jnp.concatenate(planes[p : p + 3], axis=0) for p in range(2)]
-    term = dot(columns[0], deltas[0], NT) + dot(columns[1], deltas[1], NT)
-    term_ref[...] = term * (1.0 / math.sqrt(count // 8))
+    both = jnp.concatenate(deltas, axis=0)
+    products = [dot(columns, both, NT) for columns in planes]
+    for dz in range(3):
+        term = products[dz] + pltpu.roll(products[dz + 1], 64, 1)
+        term_ref[288 * dz : 288 * dz + 288] = term * (1.0 / math.sqrt(count // 8))
     rows = jnp.concatenate([term_ref[pl.ds(ch, 27, stride=32), :] for ch in range(32)], axis=0)
-    place(rows[0:HALF].T, 0)
-    rows = jnp.concatenate([rows[HALF:864], jnp.zeros((ONE_AT - 864, 64), F32)], axis=0)
-    place(rows.T, HALF)
+    place(rows[0:HALF].T[0:64], 0)
+    rows = jnp.concatenate([rows[HALF:864], jnp.zeros((ONE_AT - 864, 128), F32)], axis=0)
+    place(rows.T[0:64], HALF)
 
     grads = []
     for p in range(-1, 3):
@@ -412,7 +416,7 @@
         functools.partial(inner_body, count),
         out_shape=tuple(jax.ShapeDtypeStruct(*x) for x in shapes.values()),
         scratch_shapes=[
-            pltpu.VMEM(shape, F32) for shape in ((864, 64), (64, 128), (4, 64, 128), (4, 128, 128))
+            pltpu.VMEM(shape, F32) for shape in ((864, 128), (64, 128), (4, 64, 128), (4, 128, 128))
         ],
         compiler_params=limit,
         cost_estimate=pl.CostEstimate(flops=2 * 10**10, bytes_accessed=2 * 10**6, transcendentals=10**6),

time: 32.3 us -> 32.2 us (level)
  no operation moved by 1% of the time
where the time goes in v1:
time: 32.2 us; the launch traced here: 31.9 us
  starting transfers between devices  15.1 us (47%)
  Pallas kernels  8.72 us (27%)
  waiting for transfers between devices  7.38 us (23%)
  between operations  0.69 us (2%)
    ppermute x4, starting transfers between devices, swap(): return lax.ppermute(block, 'space', pairs + [(t, f) for f, t in pairs])  8.98 us
    all_to_all x1, starting transfers between devices, on_device(): parts = lax.all_to_all(send, 'space', 0, 0, tiled=True)  6.06 us
    pallas_call x1, Pallas kernels, on_device(): pl.pallas_call(functools.partial(inner_body, count), out_shape=tuple((jax...  4.48 us
    ppermute x4, waiting for transfers between devices, swap(): return lax.ppermute(block, 'space', pairs + [(t, f) for f, t in pairs])  4.39 us
    pallas_call x1, Pallas kernels, on_device(): pl.pallas_call(outer_body, out_shape=(jax.ShapeDtypeStruct((1, 64, 2, cel...  2.12 us
    all_to_all x1, waiting for transfers between devices, on_device(): parts = lax.all_to_all(send, 'space', 0, 0, tiled=True)  1.82 us
    pallas_call x1, Pallas kernels, on_device(): pl.pallas_call(prepare_body, out_shape=(whole, whole, part, part, *(jax.S...  1.39 us
    ppermute x1, waiting for transfers between devices, other_core(): return lax.ppermute(block, 'dp', [(i, i ^ step) for i in range(copies)])  1.17 us
  transfers between devices with their start and end apart: 6, of which 4 were waited for; matrix products, arithmetic and copies ran while one was open for 0% of the time, Pallas kernels for 21%

profile of v1, /device:TPU:0, one launch (start us, length us, event | category | flops | bytes accessed | tf_op | source)
XLA Modules:
  0.0 31.9 jit_solution(15585414167870665508)
XLA Ops:
  0.6 1.4 %shard_map.93 = (bf16[128,256]{1,0:T(8,128)(2,1)S(1)}, bf16[128,256]{1,0:T(8,128)(2,1)S(1)}, bf16[8,512]{1,0:T(8,128)(2,1)S(1)}, bf16[8,512]{1,0:T(8,128)(2,1)S(...) custom-call(bf16[1,4,4,32,32]{4,3,2,1,0:T(8,128)(2,1)} %vol_hbm.1, ...), custom_call_target="tpu_custom_call" | custom-call | tf_op jit(solution)/shard_map/pallas_call | solution.py:379
  2.0 0.7 %collective-permute-start = (bf16[128,256]{1,0:T(8,128)(2,1)S(1)}, bf16[128,256]{1,0:T(8,128)(2,1)S(1)}, u32[]{:S(2)}, u32[]{:S(2)}) collective-permute-start(bf16[128,256]{1,0:T(8,128)(2,1)S(1)} %get-tuple-element.30.own_next_ref), channel_id=1, source_target_pairs={{2,4},{6,8},{10,12},{14,16},{18,20},{22,24},{26,28},{4,2},{8,6},{1... | collective-permute-start | bytes 196616 | tf_op jit(solution)/shard_map/ppermute | solution.py:396
  2.7 5.7 %collective-permute-start.1 = (bf16[128,256]{1,0:T(8,128)(2,1)S(1)}, bf16[128,256]{1,0:T(8,128)(2,1)S(1)}, u32[]{:S(2)}, u32[]{:S(2)}) collective-permute-start(bf16[128,256]{1,0:T(8,128)(2,1)S(1)} %get-tuple-element.31.own_near_ref), channel_id=1, source_target_pairs={{0,2},{4,6},{8,10},{12,14},{16,18},{20,22},{24,26},{28,30},{2,0},{... | collective-permute-start | bytes 196616 | tf_op jit(solution)/shard_map/ppermute | solution.py:396
  8.4 0.6 %collective-permute-start.2 = (bf16[8,512]{1,0:T(8,128)(2,1)S(1)}, bf16[8,512]{1,0:T(8,128)(2,1)S(1)}, u32[]{:S(2)}, u32[]{:S(2)}) collective-permute-start(bf16[8,512]{1,0:T(8,128)(2,1)S(1)} %get-tuple-element.37), channel_id=1, source_target_pairs={{4,8},{6,10},{12,16},{14,18},{20,24},{22,26},{8,4},{10,6},{16,12},... | collective-permute-start | bytes 24584 | tf_op jit(solution)/shard_map/ppermute | solution.py:396
  9.1 0.0 collective-permute-done.next_ref
  9.1 2.5 %collective-permute-done.1.near_ref = bf16[128,256]{1,0:T(8,128)(2,1)S(1)} collective-permute-done((bf16[128,256]{1,0:T(8,128)(2,1)S(1)}, bf16[128,256]{1,0:T(8,128)(2,1)S(1)}, u32[]{:S(2)}, u32[]{:S(2)}) %collective-permute-start.1) | collective-permute-done | bytes 65568 | tf_op jit(solution)/shard_map/ppermute | solution.py:396
  11.6 4.5 %shard_map.94 = (bf16[2,64,256]{2,1,0:T(8,128)(2,1)S(1)}, bf16[128,512]{1,0:T(8,128)(2,1)}, f32[2,32,256]{2,1,0:T(8,128)S(1)}, f32[64,1024]{1,0:T(8,128)S(1)}, f...) custom-call(bf16[128,256]{1,0:T(8,128)(2,1)S(1)} %get-tuple-element., ...), custom_call_target="tpu_custom_call" | custom-call | flops 20000000000 | bytes 2000000 | tf_op jit(solution)/shard_map/pallas_call | solution.py:415
  16.0 0.0 collective-permute-done.2.far_next_ref
  16.0 6.1 %all-to-all-start = ((bf16[16,8,512]{2,1,0:T(8,128)(2,1)}), bf16[16,8,512]{2,1,0:T(8,128)(2,1)S(1)}, u32[]{:S(2)}, u32[]{:S(2)}) async-start(bf16[16,8,512]{2,1,0:T(8,128)(2,1)} %bitcast.4), calls=%async_computation | async-start | bytes 262144 | tf_op jit(solution)/shard_map/all_to_all | solution.py:427
  22.1 1.9 %collective-permute-start.3 = (bf16[8,512]{1,0:T(8,128)(2,1)S(1)}, bf16[8,512]{1,0:T(8,128)(2,1)S(1)}, u32[]{:S(2)}, u32[]{:S(2)}) collective-permute-start(bf16[8,512]{1,0:T(8,128)(2,1)S(1)} %get-tuple-element.41), channel_id=1, source_target_pairs={{0,4},{2,6},{8,12},{10,14},{16,20},{18,22},{24,28},{26,30},{4,0},{... | collective-permute-start | bytes 24584 | tf_op jit(solution)/shard_map/ppermute | solution.py:396
  24.0 1.9 %collective-permute-done.3.far_near_ref = bf16[8,512]{1,0:T(8,128)(2,1)S(1)} collective-permute-done((bf16[8,512]{1,0:T(8,128)(2,1)S(1)}, bf16[8,512]{1,0:T(8,128)(2,1)S(1)}, u32[]{:S(2)}, u32[]{:S(2)}) %collective-permute-start.3) | collective-permute-done | bytes 8224 | tf_op jit(solution)/shard_map/ppermute | solution.py:396
  26.0 2.1 %shard_map.95 = (bf16[1,64,2,256]{3,2,1,0:T(2,128)(2,1)}, bf16[1,32,2,256]{3,2,1,0:T(2,128)(2,1)}) custom-call(bf16[8,512]{1,0:T(8,128)(2,1)S(1)} %collective-permute-done.2.far_next_ref, bf16[8,512]{1,0:T(8,128)(2,1)S(1)} %collective-permute-done.3.far_near_ref, bf16[128,256]{1,0:T(8,128)(2,1)S(1)} %collective-permute-done.next_ref, ...), custom_call_target="tpu_custom_call" | custom-call | flops 2000000000 | bytes 1000000 | tf_op jit(solution)/shard_map/pallas_call | solution.py:430
  28.1 1.8 %all-to-all-done.parts_ref = bf16[16,8,512]{2,1,0:T(8,128)(2,1)S(1)} async-done(((bf16[16,8,512]{2,1,0:T(8,128)(2,1)}), bf16[16,8,512]{2,1,0:T(8,128)(2,1)S(1)}, u32[]{:S(2)}, u32[]{:S(2)}) %all-to-all-start) | async-done | bytes 131104 | tf_op jit(solution)/shard_map/all_to_all | solution.py:427
  29.9 0.1 collective-permute-start.4
  30.0 1.2 %collective-permute-done.4.other_ref = f32[8,512]{1,0:T(8,128)S(1)} collective-permute-done((f32[8,512]{1,0:T(8,128)S(1)}, f32[8,512]{1,0:T(8,128)S(1)}, u32[]{:S(2)}, u32[]{:S(2)}) %collective-permute-start.4) | collective-permute-done | bytes 16416 | tf_op jit(solution)/shard_map/ppermute | solution.py:447
  31.2 0.7 %shard_map.97 = (f32[216]{0:T(256)}, f32[3456]{0:T(1024)}) custom-call(f32[8,512]{1,0:T(8,128)S(1)} %shard_map.96.mine_ref, f32[8,512]{1,0:T(8,128)S(1)} %collective-permute-done.4.other_ref), custom_call_target="tpu_custom_call" | custom-call | tf_op jit(solution)/shard_map/pallas_call | solution.py:454
  (1 shorter events, 0.0 us)
Async XLA Ops:
  2.0 7.1 %collective-permute-start = (bf16[128,256]{1,0:T(8,128)(2,1)S(1)}, bf16[128,256]{1,0:T(8,128)(2,1)S(1)}, u32[]{:S(2)}, u32[]{:S(2)}) collective-permute-start(bf16[128,256]{1,0:T(8,128)(2,1)S(1)} %get-tuple-element.30.own_next_ref), channel_id=1, source_target_pairs={{2,4},{6,8},{10,12},{14,16},{18,20},{22,24},{26,28},{4,2},{8,6},{1... | collective-permute-start | bytes 196616 | tf_op jit(solution)/shard_map/ppermute | solution.py:396
  2.7 8.9 %collective-permute-start.1 = (bf16[128,256]{1,0:T(8,128)(2,1)S(1)}, bf16[128,256]{1,0:T(8,128)(2,1)S(1)}, u32[]{:S(2)}, u32[]{:S(2)}) collective-permute-start(bf16[128,256]{1,0:T(8,128)(2,1)S(1)} %get-tuple-element.31.own_near_ref), channel_id=1, source_target_pairs={{0,2},{4,6},{8,10},{12,14},{16,18},{20,22},{24,26},{28,30},{2,0},{... | collective-permute-start | bytes 196616 | tf_op jit(solution)/shard_map/ppermute | solution.py:396
  8.4 7.6 %collective-permute-start.2 = (bf16[8,512]{1,0:T(8,128)(2,1)S(1)}, bf16[8,512]{1,0:T(8,128)(2,1)S(1)}, u32[]{:S(2)}, u32[]{:S(2)}) collective-permute-start(bf16[8,512]{1,0:T(8,128)(2,1)S(1)} %get-tuple-element.37), channel_id=1, source_target_pairs={{4,8},{6,10},{12,16},{14,18},{20,24},{22,26},{8,4},{10,6},{16,12},... | collective-permute-start | bytes 24584 | tf_op jit(solution)/shard_map/ppermute | solution.py:396
  16.0 13.9 %all-to-all-start = ((bf16[16,8,512]{2,1,0:T(8,128)(2,1)}), bf16[16,8,512]{2,1,0:T(8,128)(2,1)S(1)}, u32[]{:S(2)}, u32[]{:S(2)}) async-start(bf16[16,8,512]{2,1,0:T(8,128)(2,1)} %bitcast.4), calls=%async_computation | async-start | bytes 262144 | tf_op jit(solution)/shard_map/all_to_all | solution.py:427
  22.1 3.9 %collective-permute-start.3 = (bf16[8,512]{1,0:T(8,128)(2,1)S(1)}, bf16[8,512]{1,0:T(8,128)(2,1)S(1)}, u32[]{:S(2)}, u32[]{:S(2)}) collective-permute-start(bf16[8,512]{1,0:T(8,128)(2,1)S(1)} %get-tuple-element.41), channel_id=1, source_target_pairs={{0,4},{2,6},{8,12},{10,14},{16,20},{18,22},{24,28},{26,30},{4,0},{... | collective-permute-start | bytes 24584 | tf_op jit(solution)/shard_map/ppermute | solution.py:396
  29.9 1.2 %collective-permute-start.4 = (f32[8,512]{1,0:T(8,128)S(1)}, f32[8,512]{1,0:T(8,128)S(1)}, u32[]{:S(2)}, u32[]{:S(2)}) collective-permute-start(f32[8,512]{1,0:T(8,128)S(1)} %shard_map.96.mine_ref), channel_id=1, source_target_pairs={{0,1},{1,0},{2,3},{3,2},{4,5},{5,4},{6,7},{7,6},{8,9},{9,8},{10,11... | collective-permute-start | bytes 49160 | tf_op jit(solution)/shard_map/ppermute | solution.py:447

commit v2 on v1

--- a/solution.py
+++ b/solution.py
@@ -183,7 +183,7 @@
 def inner_body(
     count,
     own_next_ref, own_near_ref, next_ref, near_ref, k1_ref, k2_ref, to_kernel_ref, to_flat_ref,
-    feat_ref, send_ref, part_ref, pre_ref, act_ref, pre_two_ref, far_one_ref, far_two_ref,
+    feat_ref, send_ref, part_ref, pre_ref, act_ref, pre_two_ref, far_one_ref,
     term_ref, pair_ref, rows_ref, out_ref,
 ):
     slabs = lax.axis_size("space")
@@ -210,17 +210,26 @@
         patches.append(jnp.concatenate([*(m[16 * g : 16 * g + 16] for m in moved), rows], axis=0))
 
     k1t = k1_ref[...].astype(F32).reshape(108, 32).T.astype(BF16)
+    k2 = k2_ref[...]
     two_by_dz = jnp.concatenate(
-        [k2_ref[288 * dz : 288 * dz + 288].astype(F32).T for dz in range(3)], axis=0
+        [k2[288 * dz : 288 * dz + 256].astype(F32).T for dz in range(3)], axis=0
     ).astype(BF16)
+    nothing = jnp.zeros((288, 64), BF16)
+    ninth = []
+    for p in range(4):
+        taps = [q + 1 - p for q in range(4)]
+        taps = [k2[288 * dz + 256 : 288 * dz + 288] if 0 <= dz < 3 else nothing[0:32] for dz in taps]
+        ninth.append(jnp.concatenate(taps, axis=0).astype(F32).T)
+    ninth = jnp.concatenate(ninth, axis=0).astype(BF16)
+    back = jnp.concatenate(
+        [jnp.concatenate([k2, nothing], axis=0), jnp.concatenate([nothing, k2], axis=0)], axis=1
+    )
     banded = jnp.concatenate(
         [dot(k1t, to_kernel_ref[p], NT).astype(BF16) for p in range(4)], axis=0
     )
     far_one_ref[...] = jnp.concatenate(
         [dot(k1t, to_kernel_ref[p, 144:216], NT).astype(BF16) for p in (0, 3)], axis=0
     )
-    far_two_ref[0] = two_by_dz[0:64]
-    far_two_ref[1] = two_by_dz[128:192]
     pattern = pool_pattern()
 
     pre = dot(banded, patches[0])
@@ -245,14 +254,14 @@
 
     moved = all_shifts(pooled, half)
     planes = [jnp.concatenate([m[32 * q : 32 * q + 32] for m in moved], axis=0) for q in range(4)]
-    pre_two = [None] * 4
+    pre_two = dot(ninth, moved[8])
+    pre_two = [pre_two[64 * p : 64 * p + 64] for p in range(4)]
     for q, columns in enumerate(planes):
-        by_dz = dot(two_by_dz, columns)
+        by_dz = dot(two_by_dz, columns[0:256])
         for dz in range(3):
             p = q + 1 - dz
             if 0 <= p < 4:
-                part = by_dz[64 * dz : 64 * dz + 64]
-                pre_two[p] = part if pre_two[p] is None else pre_two[p] + part
+                pre_two[p] = pre_two[p] + by_dz[64 * dz : 64 * dz + 64]
     pre_two_ref[0], pre_two_ref[1] = pre_two[0], pre_two[3]
 
     own_cots = own_near_ref[64:128].astype(F32), own_next_ref[64:128].astype(F32)
@@ -283,12 +292,8 @@
     rows = jnp.concatenate([rows[HALF:864], jnp.zeros((ONE_AT - 864, 128), F32)], axis=0)
     place(rows.T[0:64], HALF)
 
-    grads = []
-    for p in range(-1, 3):
-        sources = [q for q in range(2) if abs(q - p) < 2]
-        taps = [k2_ref[288 * (1 + p - q) : 288 * (1 + p - q) + 288] for q in sources]
-        given = jnp.concatenate([deltas[q] for q in sources], axis=0)
-        grads.append(spread_taps(dot(jnp.concatenate(taps, axis=1), given), half))
+    taps = dot(back, both)
+    grads = [spread_taps(taps[288 * p : 288 * p + 288], half) for p in range(4)]
     part_ref[0], part_ref[1] = grads[1], grads[2]
 
     grads = jnp.where(real, jnp.concatenate(grads, axis=0), 0.0)
@@ -317,7 +322,7 @@
 
 def outer_body(
     far_next_ref, far_near_ref, next_ref, near_ref, k2_ref,
-    feat_ref, part_ref, pre_ref, act_ref, pre_two_ref, far_one_ref, far_two_ref,
+    feat_ref, part_ref, pre_ref, act_ref, pre_two_ref, far_one_ref,
     feat_out, pgrad_out,
 ):
     slabs = lax.axis_size("space")
@@ -345,7 +350,8 @@
     cots = jnp.where(odd, near, following), jnp.where(odd, following, near)
     for p in range(2):
         columns = jnp.concatenate([m[32 * p : 32 * p + 32] for m in moved], axis=0)
-        pre = pre_two_ref[p] + dot(far_two_ref[p], columns)
+        weights = k2_ref[576 * p : 576 * p + 288].astype(F32).T.astype(BF16)
+        pre = pre_two_ref[p] + dot(weights, columns)
         act, s = silu_parts(pre)
         delta = (cots[p] * (s + act * (1.0 - s))).astype(BF16)
         taps = dot(k2_ref[576 * (1 - p) : 576 * (1 - p) + 288], delta)
@@ -410,7 +416,6 @@
         "act": ((64, LANES), F32),
         "pre_two": ((2, 64, cells), F32),
         "far_one": ((64, 72), BF16),
-        "far_two": ((2, 64, 288), BF16),
     }
     feat, send, *inner = pl.pallas_call(
         functools.partial(inner_body, count),

time: 32.2 us -> 32.2 us (level)
  no operation moved by 1% of the time
where the time goes in v2:
time: 32.2 us; the launch traced here: 31.9 us
  starting transfers between devices  15.1 us (47%)
  Pallas kernels  8.76 us (27%)
  waiting for transfers between devices  7.37 us (23%)
  between operations  0.69 us (2%)
    ppermute x4, starting transfers between devices, swap(): return lax.ppermute(block, 'space', pairs + [(t, f) for f, t in pairs])  8.98 us
    all_to_all x1, starting transfers between devices, on_device(): parts = lax.all_to_all(send, 'space', 0, 0, tiled=True)  6.07 us
    pallas_call x1, Pallas kernels, on_device(): pl.pallas_call(functools.partial(inner_body, count), out_shape=tuple((jax...  4.51 us
    ppermute x4, waiting for transfers between devices, swap(): return lax.ppermute(block, 'space', pairs + [(t, f) for f, t in pairs])  4.46 us
    pallas_call x1, Pallas kernels, on_device(): pl.pallas_call(outer_body, out_shape=(jax.ShapeDtypeStruct((1, 64, 2, cel...  2.13 us
    all_to_all x1, waiting for transfers between devices, on_device(): parts = lax.all_to_all(send, 'space', 0, 0, tiled=True)  1.74 us
    pallas_call x1, Pallas kernels, on_device(): pl.pallas_call(prepare_body, out_shape=(whole, whole, part, part, *(jax.S...  1.39 us
    ppermute x1, waiting for transfers between devices, other_core(): return lax.ppermute(block, 'dp', [(i, i ^ step) for i in range(copies)])  1.17 us
  transfers between devices with their start and end apart: 6, of which 4 were waited for; matrix products, arithmetic and copies ran while one was open for 0% of the time, Pallas kernels for 21%

profile of v2, /device:TPU:0, one launch (start us, length us, event | category | flops | bytes accessed | tf_op | source)
XLA Modules:
  0.0 31.9 jit_solution(1324014315741512320)
XLA Ops:
  0.6 1.4 %shard_map.93 = (bf16[128,256]{1,0:T(8,128)(2,1)S(1)}, bf16[128,256]{1,0:T(8,128)(2,1)S(1)}, bf16[8,512]{1,0:T(8,128)(2,1)S(1)}, bf16[8,512]{1,0:T(8,128)(2,1)S(...) custom-call(bf16[1,4,4,32,32]{4,3,2,1,0:T(8,128)(2,1)} %vol_hbm.1, ...), custom_call_target="tpu_custom_call" | custom-call | tf_op jit(solution)/shard_map/pallas_call | solution.py:385
  2.0 0.7 %collective-permute-start = (bf16[128,256]{1,0:T(8,128)(2,1)S(1)}, bf16[128,256]{1,0:T(8,128)(2,1)S(1)}, u32[]{:S(2)}, u32[]{:S(2)}) collective-permute-start(bf16[128,256]{1,0:T(8,128)(2,1)S(1)} %get-tuple-element.29.own_next_ref), channel_id=1, source_target_pairs={{2,4},{6,8},{10,12},{14,16},{18,20},{22,24},{26,28},{4,2},{8,6},{1... | collective-permute-start | bytes 196616 | tf_op jit(solution)/shard_map/ppermute | solution.py:402
  2.7 5.7 %collective-permute-start.1 = (bf16[128,256]{1,0:T(8,128)(2,1)S(1)}, bf16[128,256]{1,0:T(8,128)(2,1)S(1)}, u32[]{:S(2)}, u32[]{:S(2)}) collective-permute-start(bf16[128,256]{1,0:T(8,128)(2,1)S(1)} %get-tuple-element.30.own_near_ref), channel_id=1, source_target_pairs={{0,2},{4,6},{8,10},{12,14},{16,18},{20,22},{24,26},{28,30},{2,0},{... | collective-permute-start | bytes 196616 | tf_op jit(solution)/shard_map/ppermute | solution.py:402
  8.4 0.6 %collective-permute-start.2 = (bf16[8,512]{1,0:T(8,128)(2,1)S(1)}, bf16[8,512]{1,0:T(8,128)(2,1)S(1)}, u32[]{:S(2)}, u32[]{:S(2)}) collective-permute-start(bf16[8,512]{1,0:T(8,128)(2,1)S(1)} %get-tuple-element.36), channel_id=1, source_target_pairs={{4,8},{6,10},{12,16},{14,18},{20,24},{22,26},{8,4},{10,6},{16,12},... | collective-permute-start | bytes 24584 | tf_op jit(solution)/shard_map/ppermute | solution.py:402
  9.1 0.0 collective-permute-done.next_ref
  9.1 2.5 %collective-permute-done.1.near_ref = bf16[128,256]{1,0:T(8,128)(2,1)S(1)} collective-permute-done((bf16[128,256]{1,0:T(8,128)(2,1)S(1)}, bf16[128,256]{1,0:T(8,128)(2,1)S(1)}, u32[]{:S(2)}, u32[]{:S(2)}) %collective-permute-start.1) | collective-permute-done | bytes 65568 | tf_op jit(solution)/shard_map/ppermute | solution.py:402
  11.6 4.5 %shard_map.94 = (bf16[2,64,256]{2,1,0:T(8,128)(2,1)S(1)}, bf16[128,512]{1,0:T(8,128)(2,1)}, f32[2,32,256]{2,1,0:T(8,128)S(1)}, f32[64,1024]{1,0:T(8,128)S(1)}, f...) custom-call(bf16[128,256]{1,0:T(8,128)(2,1)S(1)} %get-tuple-element.29.own_next_ref, ...), custom_call_target="tpu_custom_call" | custom-call | flops 20000000000 | bytes 2000000 | tf_op jit(solution)/shard_map/pallas_call | solution.py:420
  16.1 0.0 collective-permute-done.2.far_next_ref
  16.1 6.1 %all-to-all-start = ((bf16[16,8,512]{2,1,0:T(8,128)(2,1)}), bf16[16,8,512]{2,1,0:T(8,128)(2,1)S(1)}, u32[]{:S(2)}, u32[]{:S(2)}) async-start(bf16[16,8,512]{2,1,0:T(8,128)(2,1)} %bitcast.4), calls=%async_computation | async-start | bytes 262144 | tf_op jit(solution)/shard_map/all_to_all | solution.py:432
  22.1 1.9 %collective-permute-start.3 = (bf16[8,512]{1,0:T(8,128)(2,1)S(1)}, bf16[8,512]{1,0:T(8,128)(2,1)S(1)}, u32[]{:S(2)}, u32[]{:S(2)}) collective-permute-start(bf16[8,512]{1,0:T(8,128)(2,1)S(1)} %get-tuple-element.40), channel_id=1, source_target_pairs={{0,4},{2,6},{8,12},{10,14},{16,20},{18,22},{24,28},{26,30},{4,0},{... | collective-permute-start | bytes 24584 | tf_op jit(solution)/shard_map/ppermute | solution.py:402
  24.1 2.0 %collective-permute-done.3.far_near_ref = bf16[8,512]{1,0:T(8,128)(2,1)S(1)} collective-permute-done((bf16[8,512]{1,0:T(8,128)(2,1)S(1)}, bf16[8,512]{1,0:T(8,128)(2,1)S(1)}, u32[]{:S(2)}, u32[]{:S(2)}) %collective-permute-start.3) | collective-permute-done | bytes 8224 | tf_op jit(solution)/shard_map/ppermute | solution.py:402
  26.1 2.1 %shard_map.95 = (bf16[1,64,2,256]{3,2,1,0:T(2,128)(2,1)}, bf16[1,32,2,256]{3,2,1,0:T(2,128)(2,1)}) custom-call(bf16[8,512]{1,0:T(8,128)(2,1)S(1)} %collective-permute-done.2.far_next_ref, bf16[8,512]{1,0:T(8,128)(2,1)S(1)} %collective-permute-done.3.far_near_ref, bf16[128,256]{1,0:T(8,128)(2,1)S(1)} %collective-permute-done.next_ref, ...), custom_call_target="tpu_custom_call" | custom-call | flops 2000000000 | bytes 1000000 | tf_op jit(solution)/shard_map/pallas_call | solution.py:435
  28.2 1.7 %all-to-all-done.parts_ref = bf16[16,8,512]{2,1,0:T(8,128)(2,1)S(1)} async-done(((bf16[16,8,512]{2,1,0:T(8,128)(2,1)}), bf16[16,8,512]{2,1,0:T(8,128)(2,1)S(1)}, u32[]{:S(2)}, u32[]{:S(2)}) %all-to-all-start) | async-done | bytes 131104 | tf_op jit(solution)/shard_map/all_to_all | solution.py:432
  30.0 0.1 collective-permute-start.4
  30.0 1.2 %collective-permute-done.4.other_ref = f32[8,512]{1,0:T(8,128)S(1)} collective-permute-done((f32[8,512]{1,0:T(8,128)S(1)}, f32[8,512]{1,0:T(8,128)S(1)}, u32[]{:S(2)}, u32[]{:S(2)}) %collective-permute-start.4) | collective-permute-done | bytes 16416 | tf_op jit(solution)/shard_map/ppermute | solution.py:452
  31.2 0.7 %shard_map.97 = (f32[216]{0:T(256)}, f32[3456]{0:T(1024)}) custom-call(f32[8,512]{1,0:T(8,128)S(1)} %shard_map.96.mine_ref, f32[8,512]{1,0:T(8,128)S(1)} %collective-permute-done.4.other_ref), custom_call_target="tpu_custom_call" | custom-call | tf_op jit(solution)/shard_map/pallas_call | solution.py:459
  (1 shorter events, 0.0 us)
Async XLA Ops:
  2.0 7.1 %collective-permute-start = (bf16[128,256]{1,0:T(8,128)(2,1)S(1)}, bf16[128,256]{1,0:T(8,128)(2,1)S(1)}, u32[]{:S(2)}, u32[]{:S(2)}) collective-permute-start(bf16[128,256]{1,0:T(8,128)(2,1)S(1)} %get-tuple-element.29.own_next_ref), channel_id=1, source_target_pairs={{2,4},{6,8},{10,12},{14,16},{18,20},{22,24},{26,28},{4,2},{8,6},{1... | collective-permute-start | bytes 196616 | tf_op jit(solution)/shard_map/ppermute | solution.py:402
  2.7 8.9 %collective-permute-start.1 = (bf16[128,256]{1,0:T(8,128)(2,1)S(1)}, bf16[128,256]{1,0:T(8,128)(2,1)S(1)}, u32[]{:S(2)}, u32[]{:S(2)}) collective-permute-start(bf16[128,256]{1,0:T(8,128)(2,1)S(1)} %get-tuple-element.30.own_near_ref), channel_id=1, source_target_pairs={{0,2},{4,6},{8,10},{12,14},{16,18},{20,22},{24,26},{28,30},{2,0},{... | collective-permute-start | bytes 196616 | tf_op jit(solution)/shard_map/ppermute | solution.py:402
  8.4 7.6 %collective-permute-start.2 = (bf16[8,512]{1,0:T(8,128)(2,1)S(1)}, bf16[8,512]{1,0:T(8,128)(2,1)S(1)}, u32[]{:S(2)}, u32[]{:S(2)}) collective-permute-start(bf16[8,512]{1,0:T(8,128)(2,1)S(1)} %get-tuple-element.36), channel_id=1, source_target_pairs={{4,8},{6,10},{12,16},{14,18},{20,24},{22,26},{8,4},{10,6},{16,12},... | collective-permute-start | bytes 24584 | tf_op jit(solution)/shard_map/ppermute | solution.py:402
  16.1 13.9 %all-to-all-start = ((bf16[16,8,512]{2,1,0:T(8,128)(2,1)}), bf16[16,8,512]{2,1,0:T(8,128)(2,1)S(1)}, u32[]{:S(2)}, u32[]{:S(2)}) async-start(bf16[16,8,512]{2,1,0:T(8,128)(2,1)} %bitcast.4), calls=%async_computation | async-start | bytes 262144 | tf_op jit(solution)/shard_map/all_to_all | solution.py:432
  22.1 3.9 %collective-permute-start.3 = (bf16[8,512]{1,0:T(8,128)(2,1)S(1)}, bf16[8,512]{1,0:T(8,128)(2,1)S(1)}, u32[]{:S(2)}, u32[]{:S(2)}) collective-permute-start(bf16[8,512]{1,0:T(8,128)(2,1)S(1)} %get-tuple-element.40), channel_id=1, source_target_pairs={{0,4},{2,6},{8,12},{10,14},{16,20},{18,22},{24,28},{26,30},{4,0},{... | collective-permute-start | bytes 24584 | tf_op jit(solution)/shard_map/ppermute | solution.py:402
  30.0 1.2 %collective-permute-start.4 = (f32[8,512]{1,0:T(8,128)S(1)}, f32[8,512]{1,0:T(8,128)S(1)}, u32[]{:S(2)}, u32[]{:S(2)}) collective-permute-start(f32[8,512]{1,0:T(8,128)S(1)} %shard_map.96.mine_ref), channel_id=1, source_target_pairs={{0,1},{1,0},{2,3},{3,2},{4,5},{5,4},{6,7},{7,6},{8,9},{9,8},{10,11... | collective-permute-start | bytes 49160 | tf_op jit(solution)/shard_map/ppermute | solution.py:452

commit v3 on v1

--- a/solution.py
+++ b/solution.py
@@ -183,8 +183,8 @@
 def inner_body(
     count,
     own_next_ref, own_near_ref, next_ref, near_ref, k1_ref, k2_ref, to_kernel_ref, to_flat_ref,
-    feat_ref, send_ref, part_ref, pre_ref, act_ref, pre_two_ref, far_one_ref, far_two_ref,
-    term_ref, pair_ref, rows_ref, out_ref,
+    feat_ref, send_hbm, part_ref, pre_ref, act_ref, pre_two_ref, far_one_ref, far_two_ref,
+    term_ref, pair_ref, rows_ref, out_ref, rounded_ref, sems,
 ):
     slabs = lax.axis_size("space")
     me = lax.axis_index("space")
@@ -282,6 +282,16 @@
     place(rows[0:HALF].T[0:64], 0)
     rows = jnp.concatenate([rows[HALF:864], jnp.zeros((ONE_AT - 864, 128), F32)], axis=0)
     place(rows.T[0:64], HALF)
+
+    def leave(first, last, sem):
+        for tile in range(first, last):
+            rounded_ref[:, 128 * tile : 128 * tile + 128] = out_ref[tile].astype(BF16)
+        lanes = pl.ds(128 * first, 128 * (last - first))
+        copy = pltpu.make_async_copy(rounded_ref.at[:, lanes], send_hbm.at[:, lanes], sem)
+        copy.start()
+        return copy
+
+    copies = [leave(0, 3, sems.at[0])]
 
     grads = []
     for p in range(-1, 3):
@@ -311,8 +321,9 @@
     lane = lax.broadcasted_iota(jnp.int32, rows.shape, 1)
     pair = jnp.where(lane < 64, rounded, pltpu.roll(rows - rounded, 64, 1))
     place(pair, ONE_AT)
-    for tile in range(4):
-        send_ref[:, 128 * tile : 128 * tile + 128] = out_ref[tile].astype(BF16)
+    copies.append(leave(3, 4, sems.at[1]))
+    for copy in copies:
+        copy.wait()
 
 
 def outer_body(
@@ -415,15 +426,19 @@
     feat, send, *inner = pl.pallas_call(
         functools.partial(inner_body, count),
         out_shape=tuple(jax.ShapeDtypeStruct(*x) for x in shapes.values()),
+        out_specs=tuple(
+            pl.BlockSpec(memory_space=pltpu.HBM if name == "send" else pltpu.VMEM) for name in shapes
+        ),
         scratch_shapes=[
-            pltpu.VMEM(shape, F32) for shape in ((864, 128), (64, 128), (4, 64, 128), (4, 128, 128))
+            *(pltpu.VMEM(x, F32) for x in ((864, 128), (64, 128), (4, 64, 128), (4, 128, 128))),
+            pltpu.VMEM((128, HALF), BF16),
+            pltpu.SemaphoreType.DMA((2,)),
         ],
         compiler_params=limit,
         cost_estimate=pl.CostEstimate(flops=2 * 10**10, bytes_accessed=2 * 10**6, transcendentals=10**6),
     )(to_next, to_near, following, near, *weights)
     share = 64 // slabs
     send, far_next = lax.optimization_barrier((send.reshape(slabs, 2 * share, HALF), far_next))
-    send = pltpu.with_memory_space_constraint(send, pltpu.VMEM)
     parts = lax.all_to_all(send, "space", 0, 0, tiled=True)
     _, to_far_near = lax.optimization_barrier((send, to_far_near))
     far_near = swap(to_far_near, [(i, i + 2) for i in fours])

time: 32.2 us -> 32.2 us (level)
  no operation moved by 1% of the time
where the time goes in v3:
time: 32.2 us; the launch traced here: 31.9 us
  starting transfers between devices  15.1 us (47%)
  Pallas kernels  8.75 us (27%)
  waiting for transfers between devices  7.38 us (23%)
  between operations  0.7 us (2%)
    ppermute x4, starting transfers between devices, swap(): return lax.ppermute(block, 'space', pairs + [(t, f) for f, t in pairs])  8.98 us
    all_to_all x1, starting transfers between devices, on_device(): parts = lax.all_to_all(send, 'space', 0, 0, tiled=True)  6.07 us
    pallas_call x1, Pallas kernels, on_device(): pl.pallas_call(functools.partial(inner_body, count), out_shape=tuple((jax...  4.51 us
    ppermute x4, waiting for transfers between devices, swap(): return lax.ppermute(block, 'space', pairs + [(t, f) for f, t in pairs])  4.46 us
    pallas_call x1, Pallas kernels, on_device(): pl.pallas_call(outer_body, out_shape=(jax.ShapeDtypeStruct((1, 64, 2, cel...  2.12 us
    all_to_all x1, waiting for transfers between devices, on_device(): parts = lax.all_to_all(send, 'space', 0, 0, tiled=True)  1.75 us
    pallas_call x1, Pallas kernels, on_device(): pl.pallas_call(prepare_body, out_shape=(whole, whole, part, part, *(jax.S...  1.39 us
    ppermute x1, waiting for transfers between devices, other_core(): return lax.ppermute(block, 'dp', [(i, i ^ step) for i in range(copies)])  1.17 us
  transfers between devices with their start and end apart: 6, of which 4 were waited for; matrix products, arithmetic and copies ran while one was open for 0% of the time, Pallas kernels for 21%

profile of v3, /device:TPU:0, one launch (start us, length us, event | category | flops | bytes accessed | tf_op | source)
XLA Modules:
  0.0 31.9 jit_solution(5562030601806522131)
XLA Ops:
  0.6 1.4 %shard_map.93 = (bf16[128,256]{1,0:T(8,128)(2,1)S(1)}, bf16[128,256]{1,0:T(8,128)(2,1)S(1)}, bf16[8,512]{1,0:T(8,128)(2,1)S(1)}, bf16[8,512]{1,0:T(8,128)(2,1)S(...) custom-call(bf16[1,4,4,32,32]{4,3,2,1,0:T(8,128)(2,1)} %vol_hbm.1, ...), custom_call_target="tpu_custom_call" | custom-call | tf_op jit(solution)/shard_map/pallas_call | solution.py:390
  2.0 0.7 %collective-permute-start = (bf16[128,256]{1,0:T(8,128)(2,1)S(1)}, bf16[128,256]{1,0:T(8,128)(2,1)S(1)}, u32[]{:S(2)}, u32[]{:S(2)}) collective-permute-start(bf16[128,256]{1,0:T(8,128)(2,1)S(1)} %get-tuple-element.30.own_next_ref), channel_id=1, source_target_pairs={{2,4},{6,8},{10,12},{14,16},{18,20},{22,24},{26,28},{4,2},{8,6},{1... | collective-permute-start | bytes 196616 | tf_op jit(solution)/shard_map/ppermute | solution.py:407
  2.7 5.7 %collective-permute-start.1 = (bf16[128,256]{1,0:T(8,128)(2,1)S(1)}, bf16[128,256]{1,0:T(8,128)(2,1)S(1)}, u32[]{:S(2)}, u32[]{:S(2)}) collective-permute-start(bf16[128,256]{1,0:T(8,128)(2,1)S(1)} %get-tuple-element.31.own_near_ref), channel_id=1, source_target_pairs={{0,2},{4,6},{8,10},{12,14},{16,18},{20,22},{24,26},{28,30},{2,0},{... | collective-permute-start | bytes 196616 | tf_op jit(solution)/shard_map/ppermute | solution.py:407
  8.4 0.6 %collective-permute-start.2 = (bf16[8,512]{1,0:T(8,128)(2,1)S(1)}, bf16[8,512]{1,0:T(8,128)(2,1)S(1)}, u32[]{:S(2)}, u32[]{:S(2)}) collective-permute-start(bf16[8,512]{1,0:T(8,128)(2,1)S(1)} %get-tuple-element.37), channel_id=1, source_target_pairs={{4,8},{6,10},{12,16},{14,18},{20,24},{22,26},{8,4},{10,6},{16,12},... | collective-permute-start | bytes 24584 | tf_op jit(solution)/shard_map/ppermute | solution.py:407
  9.1 0.0 collective-permute-done.next_ref
  9.1 2.5 %collective-permute-done.1.near_ref = bf16[128,256]{1,0:T(8,128)(2,1)S(1)} collective-permute-done((bf16[128,256]{1,0:T(8,128)(2,1)S(1)}, bf16[128,256]{1,0:T(8,128)(2,1)S(1)}, u32[]{:S(2)}, u32[]{:S(2)}) %collective-permute-start.1) | collective-permute-done | bytes 65568 | tf_op jit(solution)/shard_map/ppermute | solution.py:407
  11.6 4.5 %shard_map.94 = (bf16[2,64,256]{2,1,0:T(8,128)(2,1)S(1)}, bf16[128,512]{1,0:T(8,128)(2,1)}, f32[2,32,256]{2,1,0:T(8,128)S(1)}, f32[64,1024]{1,0:T(8,128)S(1)}, f...) custom-call(bf16[128,256]{1,0:T(8,128)(2,1)S(1)} %get-tuple-element., ...), custom_call_target="tpu_custom_call" | custom-call | flops 20000000000 | bytes 2000000 | tf_op jit(solution)/shard_map/pallas_call | solution.py:426
  16.1 0.0 collective-permute-done.2.far_next_ref
  16.1 6.1 %all-to-all-start = ((bf16[16,8,512]{2,1,0:T(8,128)(2,1)}), bf16[16,8,512]{2,1,0:T(8,128)(2,1)S(1)}, u32[]{:S(2)}, u32[]{:S(2)}) async-start(bf16[16,8,512]{2,1,0:T(8,128)(2,1)} %bitcast.4), calls=%async_computation | async-start | bytes 262144 | tf_op jit(solution)/shard_map/all_to_all | solution.py:442
  22.2 1.9 %collective-permute-start.3 = (bf16[8,512]{1,0:T(8,128)(2,1)S(1)}, bf16[8,512]{1,0:T(8,128)(2,1)S(1)}, u32[]{:S(2)}, u32[]{:S(2)}) collective-permute-start(bf16[8,512]{1,0:T(8,128)(2,1)S(1)} %get-tuple-element.41), channel_id=1, source_target_pairs={{0,4},{2,6},{8,12},{10,14},{16,20},{18,22},{24,28},{26,30},{4,0},{... | collective-permute-start | bytes 24584 | tf_op jit(solution)/shard_map/ppermute | solution.py:407
  24.1 2.0 %collective-permute-done.3.far_near_ref = bf16[8,512]{1,0:T(8,128)(2,1)S(1)} collective-permute-done((bf16[8,512]{1,0:T(8,128)(2,1)S(1)}, bf16[8,512]{1,0:T(8,128)(2,1)S(1)}, u32[]{:S(2)}, u32[]{:S(2)}) %collective-permute-start.3) | collective-permute-done | bytes 8224 | tf_op jit(solution)/shard_map/ppermute | solution.py:407
  26.1 2.1 %shard_map.95 = (bf16[1,64,2,256]{3,2,1,0:T(2,128)(2,1)}, bf16[1,32,2,256]{3,2,1,0:T(2,128)(2,1)}) custom-call(bf16[8,512]{1,0:T(8,128)(2,1)S(1)} %collective-permute-done.2.far_next_ref, bf16[8,512]{1,0:T(8,128)(2,1)S(1)} %collective-permute-done.3.far_near_ref, bf16[128,256]{1,0:T(8,128)(2,1)S(1)} %collective-permute-done.next_ref, ...), custom_call_target="tpu_custom_call" | custom-call | flops 2000000000 | bytes 1000000 | tf_op jit(solution)/shard_map/pallas_call | solution.py:445
  28.2 1.7 %all-to-all-done.parts_ref = bf16[16,8,512]{2,1,0:T(8,128)(2,1)S(1)} async-done(((bf16[16,8,512]{2,1,0:T(8,128)(2,1)}), bf16[16,8,512]{2,1,0:T(8,128)(2,1)S(1)}, u32[]{:S(2)}, u32[]{:S(2)}) %all-to-all-start) | async-done | bytes 131104 | tf_op jit(solution)/shard_map/all_to_all | solution.py:442
  30.0 0.1 collective-permute-start.4
  30.1 1.2 %collective-permute-done.4.other_ref = f32[8,512]{1,0:T(8,128)S(1)} collective-permute-done((f32[8,512]{1,0:T(8,128)S(1)}, f32[8,512]{1,0:T(8,128)S(1)}, u32[]{:S(2)}, u32[]{:S(2)}) %collective-permute-start.4) | collective-permute-done | bytes 16416 | tf_op jit(solution)/shard_map/ppermute | solution.py:462
  31.2 0.7 %shard_map.97 = (f32[216]{0:T(256)}, f32[3456]{0:T(1024)}) custom-call(f32[8,512]{1,0:T(8,128)S(1)} %shard_map.96.mine_ref, f32[8,512]{1,0:T(8,128)S(1)} %collective-permute-done.4.other_ref), custom_call_target="tpu_custom_call" | custom-call | tf_op jit(solution)/shard_map/pallas_call | solution.py:469
  (1 shorter events, 0.0 us)
Async XLA Ops:
  2.0 7.1 %collective-permute-start = (bf16[128,256]{1,0:T(8,128)(2,1)S(1)}, bf16[128,256]{1,0:T(8,128)(2,1)S(1)}, u32[]{:S(2)}, u32[]{:S(2)}) collective-permute-start(bf16[128,256]{1,0:T(8,128)(2,1)S(1)} %get-tuple-element.30.own_next_ref), channel_id=1, source_target_pairs={{2,4},{6,8},{10,12},{14,16},{18,20},{22,24},{26,28},{4,2},{8,6},{1... | collective-permute-start | bytes 196616 | tf_op jit(solution)/shard_map/ppermute | solution.py:407
  2.7 8.9 %collective-permute-start.1 = (bf16[128,256]{1,0:T(8,128)(2,1)S(1)}, bf16[128,256]{1,0:T(8,128)(2,1)S(1)}, u32[]{:S(2)}, u32[]{:S(2)}) collective-permute-start(bf16[128,256]{1,0:T(8,128)(2,1)S(1)} %get-tuple-element.31.own_near_ref), channel_id=1, source_target_pairs={{0,2},{4,6},{8,10},{12,14},{16,18},{20,22},{24,26},{28,30},{2,0},{... | collective-permute-start | bytes 196616 | tf_op jit(solution)/shard_map/ppermute | solution.py:407
  8.4 7.6 %collective-permute-start.2 = (bf16[8,512]{1,0:T(8,128)(2,1)S(1)}, bf16[8,512]{1,0:T(8,128)(2,1)S(1)}, u32[]{:S(2)}, u32[]{:S(2)}) collective-permute-start(bf16[8,512]{1,0:T(8,128)(2,1)S(1)} %get-tuple-element.37), channel_id=1, source_target_pairs={{4,8},{6,10},{12,16},{14,18},{20,24},{22,26},{8,4},{10,6},{16,12},... | collective-permute-start | bytes 24584 | tf_op jit(solution)/shard_map/ppermute | solution.py:407
  16.1 13.9 %all-to-all-start = ((bf16[16,8,512]{2,1,0:T(8,128)(2,1)}), bf16[16,8,512]{2,1,0:T(8,128)(2,1)S(1)}, u32[]{:S(2)}, u32[]{:S(2)}) async-start(bf16[16,8,512]{2,1,0:T(8,128)(2,1)} %bitcast.4), calls=%async_computation | async-start | bytes 262144 | tf_op jit(solution)/shard_map/all_to_all | solution.py:442
  22.2 3.9 %collective-permute-start.3 = (bf16[8,512]{1,0:T(8,128)(2,1)S(1)}, bf16[8,512]{1,0:T(8,128)(2,1)S(1)}, u32[]{:S(2)}, u32[]{:S(2)}) collective-permute-start(bf16[8,512]{1,0:T(8,128)(2,1)S(1)} %get-tuple-element.41), channel_id=1, source_target_pairs={{0,4},{2,6},{8,12},{10,14},{16,20},{18,22},{24,28},{26,30},{4,0},{... | collective-permute-start | bytes 24584 | tf_op jit(solution)/shard_map/ppermute | solution.py:407
  30.0 1.2 %collective-permute-start.4 = (f32[8,512]{1,0:T(8,128)S(1)}, f32[8,512]{1,0:T(8,128)S(1)}, u32[]{:S(2)}, u32[]{:S(2)}) collective-permute-start(f32[8,512]{1,0:T(8,128)S(1)} %shard_map.96.mine_ref), channel_id=1, source_target_pairs={{0,1},{1,0},{2,3},{3,2},{4,5},{5,4},{6,7},{7,6},{8,9},{9,8},{10,11... | collective-permute-start | bytes 49160 | tf_op jit(solution)/shard_map/ppermute | solution.py:462
